TPU v7x, 32 devices: a whole 2x2x4 slice. The times are simulated.
32 devices in a mesh: dst: 8 (over z, y), src: 4 (over x, core).
Axes of the slice: x: 2, y: 2, z: 4, core: 2. Of those that a mesh axis runs over, the one named last changes fastest.
Arguments:
- transitions: bfloat16 [2048, 128, 128], P(('dst', 'src')), may hold values from 0.0009994507 to 1
- row_block: int32 [2048], P(('dst', 'src')), may hold values from -1 to 1023, as said below
- col_block: int32 [2048], P(('dst', 'src')), may hold values from -1 to 1023, as said below
- beta_last: float32 [32, 256, 4, 128], P(None, 'dst', 'src'), may hold values from 0.2 to 2
- emissions: bfloat16 [2, 32, 256, 4, 128], P(None, None, 'dst', 'src'), may hold values from 0.019897461 to 1
- forward: bfloat16 [2, 32, 256, 4, 128], P(None, None, 'dst', 'src'), may hold values from 0.03 to 125, as said below
Outputs:
- counts: bfloat16 [2048, 128, 128], P(('dst', 'src'))
- beta_first: float32 [32, 256, 4, 128], P(None, 'dst', 'src')
- log_norms: float32 [2, 32], replicated
Inputs may be any that keep to these rules, and one draw needn't show every extreme that they name: `row_block`: slots are grouped by device (index dst * 4 + src), 64 to a device. A live slot holds a block whose source block number r has r % 4 equal to the device's src index and whose destination block lies in the device's dst index's own consecutive equal share of blocks; no block appears twice; live slots come first, and empty ones hold -1 in both arrays. One device has all 64 slots live; each device has at least one. `col_block`: same slots as row_block; -1 exactly where row_block is -1. `forward`: Positive.
All inputs are finite; a program needn't handle non-finite values.
Results may differ from a plain program's by a relative error of at most 0.0029.
Values may be sent and summed in bfloat16 or wider, within the bound.
A program may use at most 64 MiB of HBM per device.

v0:
```python
import functools

import jax
import jax.numpy as jnp
from jax import lax
from jax.experimental import pallas as pl
from jax.experimental.pallas import tpu as pltpu
from jax.sharding import PartitionSpec as P

MESH = pl.DeviceIdType.MESH


def kernel(nd, ns, total_states, table,
           trans, msg0, em1, fwd, counts, beta, scales,
           msgs0, msgs1, fwds0, fwds1, run, parts, ypart, zsend, zpart, tdst, tsrc,
           send_m, recv_m, send_f, recv_f, send_y, recv_y, send_z, recv_z,
           send_td, recv_td, send_ts, recv_ts):
    local, seqs, blk = msg0.shape
    slots = trans.shape[0]
    nz, nx = nd // 2, ns // 2
    me_d, me_s = lax.axis_index("dst"), lax.axis_index("src")
    z, y = me_d // 2, me_d % 2
    x, core = me_s // 2, me_s % 2

    def at_dst(d):
        return (d, me_s)

    def at_src(s):
        return (me_d, s)

    def copy(src, dst, ssem, rsem, dev):
        return pltpu.make_async_remote_copy(
            src_ref=src, dst_ref=dst, send_sem=ssem, recv_sem=rsem,
            device_id=dev, device_id_type=MESH)

    barrier = pltpu.get_barrier_semaphore()
    for o in range(1, nd):
        pl.semaphore_signal(barrier, inc=1, device_id=at_dst((me_d + o) % nd), device_id_type=MESH)
    for o in range(1, ns):
        pl.semaphore_signal(barrier, inc=1, device_id=at_src((me_s + o) % ns), device_id_type=MESH)
    pl.semaphore_wait(barrier, nd + ns - 2)

    msgs, fwds = (msgs0, msgs1), (fwds0, fwds1)
    pending = []

    def other(pos, o):
        for bit in range(o.bit_length()):
            if o >> bit & 1:
                pos = pos + (1 << bit) - 2 * (pos // (1 << bit) % 2) * (1 << bit)
        return pos

    def gather_side(buf, k, me, side_dev, ssem, rsem):
        c = copy(buf[k].at[me], buf[k].at[me], ssem.at[k, 0], rsem.at[k, me], side_dev)
        c.start()
        pending.append(c)

    def gather_line(buf, k, me, count, dev, ssem, rsem):
        pos, side = me // 2, me % 2
        for o in range(1, count):
            c = copy(buf[k].at[me], buf[k].at[me], ssem.at[k, o], rsem.at[k, me],
                     dev(other(pos, o) * 2 + side))
            c.start()
            pending.append(c)

    def gather_pass(buf, k, me, offsets, count, side_dev, ssem, rsem):
        pos, side = me // 2, me % 2
        for o in offsets:
            e = other(pos, o) * 2 + side
            c = copy(buf[k].at[e], buf[k].at[e], ssem.at[k, count + o - 1], rsem.at[k, e], side_dev)
            c.wait_recv()
            c.start()
            pending.append(c)

    def gather_end(buf, k, me, count, side_dev, ssem, rsem):
        pos, side = me // 2, me % 2
        for o in range(count):
            e = other(pos, o) * 2 + 1 - side
            copy(buf[k].at[e], buf[k].at[e], ssem.at[k, 0], rsem.at[k, e], side_dev).wait_recv()

    mate_d = at_dst(z * 2 + 1 - y)
    mate_s = at_src(x * 2 + 1 - core)

    def message_gather(k):
        gather_line(msgs, k, me_s, nx, at_src, send_m, recv_m)
        gather_side(msgs, k, me_s, mate_s, send_m, recv_m)

    def message_arrive(k):
        gather_pass(msgs, k, me_s, range(1, nx), nx, mate_s, send_m, recv_m)
        gather_end(msgs, k, me_s, nx, mate_s, send_m, recv_m)

    def forward_pass(k, offsets):
        gather_pass(fwds, k, me_d, offsets, nz, mate_d, send_f, recv_f)

    def products(k):
        run[0] = jnp.zeros((seqs, blk), jnp.float32)

        def one(j, carry):
            c = table[slots + j]
            block = msgs[k][c // local, c % local]
            run[j + 1] = lax.dot_general(block, trans[table[j]], (((1,), (1,)), ((), ())),
                                         preferred_element_type=jnp.float32)
            return carry

        lax.fori_loop(0, slots, one, 0, unroll=8)

        def add_run(j, acc):
            acc = run[j + 1] + acc * table[2 * slots + j].astype(jnp.float32)
            run[j + 1] = acc
            return acc

        lax.fori_loop(0, slots, add_run, jnp.zeros((seqs, blk), jnp.float32), unroll=4)

        for d in range(nd):
            def put(a, carry, d=d):
                parts[k, d, a] = run[table[6 * slots + d * local + a]].astype(jnp.bfloat16)
                return carry

            lax.fori_loop(0, local, put, 0, unroll=4)

    def reduce_side(k):
        for o in reversed(range(nz)):
            zt = other(z, o)
            c = copy(parts.at[k, zt * 2 + 1 - y], ypart.at[k, zt], send_y.at[k, o],
                     recv_y.at[k, zt], mate_d)
            c.start()
            pending.append(c)

    def reduce_line(k):
        for o in reversed(range(1, nz)):
            zt = other(z, o)
            copy(parts.at[k, zt * 2 + 1 - y], ypart.at[k, zt], send_y.at[k, o],
                 recv_y.at[k, zt], mate_d).wait_recv()

            def add(a, carry):
                zsend[k, zt, a] = (parts[k, zt * 2 + y, a].astype(jnp.float32)
                                   + ypart[k, zt, a].astype(jnp.float32)).astype(jnp.bfloat16)
                return carry

            lax.fori_loop(0, local, add, 0, unroll=4)
            c = copy(zsend.at[k, zt], zpart.at[k, z], send_z.at[k, o - 1], recv_z.at[k, z],
                     at_dst(zt * 2 + y))
            c.start()
            pending.append(c)

    def reduce_end(k):
        copy(parts.at[k, z * 2 + 1 - y], ypart.at[k, z], send_y.at[k, 0],
             recv_y.at[k, z], mate_d).wait_recv()
        for o in range(1, nz):
            zf = other(z, o)
            copy(zsend.at[k, zf], zpart.at[k, zf], send_z.at[k, o - 1], recv_z.at[k, zf],
                 mate_d).wait_recv()

        def add(a, total):
            raw = parts[k, me_d, a].astype(jnp.float32) + ypart[k, z, a].astype(jnp.float32)
            for o in range(1, nz):
                raw = raw + zpart[k, other(z, o), a].astype(jnp.float32)
            beta[a] = raw
            if k == 0:
                msgs[1][me_s, a] = (em1[a].astype(jnp.float32) * raw).astype(jnp.bfloat16)
            return total + fwd[k, a].astype(jnp.float32) * raw

        total = lax.fori_loop(0, local, add, jnp.zeros((seqs, blk), jnp.float32), unroll=2)
        tdst[me_d, pl.ds(k * seqs, seqs)] = total

    def keep_message(a, carry):
        msgs[0][me_s, a] = msg0[a]
        return carry

    lax.fori_loop(0, local, keep_message, 0, unroll=4)
    message_gather(0)
    for k in range(2):
        def keep_forward(a, carry, k=k):
            fwds[k][me_d, a] = fwd[k, a]
            return carry

        lax.fori_loop(0, local, keep_forward, 0, unroll=4)
    gather_line(fwds, 0, me_d, nz, at_dst, send_f, recv_f)
    gather_side(fwds, 0, me_d, mate_d, send_f, recv_f)
    message_arrive(0)
    forward_pass(0, range(1, 2))
    products(0)
    reduce_side(0)
    reduce_line(0)
    forward_pass(0, range(2, nz))
    gather_side(fwds, 1, me_d, mate_d, send_f, recv_f)
    gather_line(fwds, 1, me_d, nz, at_dst, send_f, recv_f)
    reduce_end(0)

    message_gather(1)
    message_arrive(1)
    forward_pass(1, range(1, 2))
    products(1)
    reduce_side(1)
    reduce_line(1)
    forward_pass(1, range(2, nz))
    reduce_end(1)

    for o in range(1, nd):
        c = copy(tdst.at[me_d], tdst.at[me_d], send_td.at[o - 1], recv_td.at[me_d],
                 at_dst((me_d + o) % nd))
        c.start()
        pending.append(c)
    for o in range(1, nd):
        e = (me_d + o) % nd
        copy(tdst.at[e], tdst.at[e], send_td.at[o - 1], recv_td.at[e], at_dst(e)).wait_recv()
    tsrc[me_s] = sum(tdst[d] for d in range(nd))
    for o in range(1, ns):
        c = copy(tsrc.at[me_s], tsrc.at[me_s], send_ts.at[o - 1], recv_ts.at[me_s],
                 at_src((me_s + o) % ns))
        c.start()
        pending.append(c)
    for o in range(1, ns):
        e = (me_s + o) % ns
        copy(tsrc.at[e], tsrc.at[e], send_ts.at[o - 1], recv_ts.at[e], at_src(e)).wait_recv()
    whole = sum(tsrc[s] for s in range(ns))
    norm = jnp.sum(whole, axis=1, keepdims=True) / total_states
    norm = jnp.broadcast_to(norm, (2 * seqs, blk))
    scales[...] = norm
    inverse = 1.0 / norm

    def finish(a, carry):
        beta[a] = beta[a] / norm[seqs:]
        return carry

    lax.fori_loop(0, local, finish, 0)

    for k in range(2):
        gather_end(fwds, k, me_d, nz, mate_d, send_f, recv_f)

    def count(m, carry):
        r, c = table[3 * slots + m], table[4 * slots + m]
        left = jnp.concatenate([fwds[k][r // local, r % local] for k in range(2)], axis=0)
        right = jnp.concatenate([msgs[k][c // local, c % local] for k in range(2)], axis=0)
        right = (right.astype(jnp.float32) * inverse).astype(jnp.bfloat16)
        value = lax.dot_general(left, right, (((0,), (0,)), ((), ())),
                                preferred_element_type=jnp.float32)
        counts[m] = (value * trans[m].astype(jnp.float32) * table[5 * slots + m].astype(jnp.float32)).astype(jnp.bfloat16)
        return carry

    lax.fori_loop(0, slots, count, 0, unroll=4)
    for c in pending:
        c.wait_send()


def body(nd, ns, transitions, row_block, col_block, beta_last, emissions, forward):
    seqs, local, _, blk = beta_last.shape
    slots = transitions.shape[0]
    columns, rows = local * ns, local * nd
    total_states = rows * ns * blk

    live = row_block >= 0
    row = jnp.where(live, row_block // ns, 0)
    col = jnp.where(live, col_block % columns, 0)
    col = col % ns * local + col // ns
    key = jnp.where(live, row, rows)
    number = jnp.arange(slots)
    before = (key[None, :] < key[:, None]) | (
        (key[None, :] == key[:, None]) & (number[None, :] < number[:, None]))
    rank = jnp.sum(before.astype(jnp.int32), axis=1)
    place = (rank[None, :] == number[:, None]).astype(jnp.int32)
    perm = jnp.sum(place * number[None, :].astype(jnp.int32), axis=1)
    pcol = jnp.sum(place * col[None, :], axis=1)
    same = jnp.any((key[None, :] == key[:, None]) & (rank[None, :] == rank[:, None] - 1), axis=1)
    flag = jnp.sum(place * same[None, :].astype(jnp.int32), axis=1)
    every = jnp.arange(rows)
    last = jnp.where(jnp.any(key[None, :] == every[:, None], axis=1),
                     jnp.sum((key[None, :] <= every[:, None]).astype(jnp.int32), axis=1), 0)

    table = jnp.concatenate(
        [perm, pcol, flag, row, col, live.astype(jnp.int32), last]).astype(jnp.int32)

    def by_block(array):
        return jnp.swapaxes(array[..., 0, :], -3, -2)

    msg0 = by_block((emissions[0].astype(jnp.float32) * beta_last).astype(jnp.bfloat16))
    em1 = by_block(emissions[1])
    fwd = by_block(forward)

    smem = pl.BlockSpec(memory_space=pltpu.SMEM)
    vmem = pl.BlockSpec(memory_space=pltpu.VMEM)
    nz, nx = nd // 2, ns // 2
    block = (local, seqs, blk)
    dma = pltpu.SemaphoreType.DMA
    counts, beta, scales = pl.pallas_call(
        functools.partial(kernel, nd, ns, float(total_states)),
        out_shape=(
            jax.ShapeDtypeStruct(transitions.shape, jnp.bfloat16),
            jax.ShapeDtypeStruct(block, jnp.float32),
            jax.ShapeDtypeStruct((2 * seqs, blk), jnp.float32),
        ),
        in_specs=[smem] + [vmem] * 4,
        out_specs=(vmem, vmem, vmem),
        scratch_shapes=[
            pltpu.VMEM((ns,) + block, jnp.bfloat16),
            pltpu.VMEM((ns,) + block, jnp.bfloat16),
            pltpu.VMEM((nd,) + block, jnp.bfloat16),
            pltpu.VMEM((nd,) + block, jnp.bfloat16),
            pltpu.VMEM((slots + 1, seqs, blk), jnp.float32),
            pltpu.VMEM((2, nd) + block, jnp.bfloat16),
            pltpu.VMEM((2, nz) + block, jnp.bfloat16),
            pltpu.VMEM((2, nz) + block, jnp.bfloat16),
            pltpu.VMEM((2, nz) + block, jnp.bfloat16),
            pltpu.VMEM((nd, 2 * seqs, blk), jnp.float32),
            pltpu.VMEM((ns, 2 * seqs, blk), jnp.float32),
            dma((2, 2 * nx)), dma((2, ns)),
            dma((2, 2 * nz)), dma((2, nd)),
            dma((2, nz)), dma((2, nz)),
            dma((2, nz)), dma((2, nz)),
            dma((nd,)), dma((nd,)),
            dma((ns,)), dma((ns,)),
        ],
        compiler_params=pltpu.CompilerParams(
            collective_id=0, has_side_effects=True, vmem_limit_bytes=48 * 1024 * 1024),
    )(table, transitions, msg0, em1, fwd)
    first, second = scales[:seqs, 0], scales[seqs:, 0]
    logs = jnp.log(jnp.stack([first, second / first]))
    return counts, jnp.swapaxes(beta, 0, 1)[:, :, None, :], logs


def solution(mesh):
    return jax.shard_map(
        functools.partial(body, mesh.shape["dst"], mesh.shape["src"]),
        mesh=mesh,
        in_specs=(
            P(("dst", "src"), None, None),
            P(("dst", "src")),
            P(("dst", "src")),
            P(None, "dst", "src", None),
            P(None, None, "dst", "src", None),
            P(None, None, "dst", "src", None),
        ),
        out_specs=(P(("dst", "src"), None, None), P(None, "dst", "src", None), P()),
        check_vma=False,
    )
```

profile of v0, /device:TPU:0, one launch (start us, length us, event | category | flops | bytes accessed | tf_op | source)
XLA Modules:
  0.0 124.8 jit_solution(3423660001860092838)
XLA Ops:
  0.6 0.0 copy-start.1
  0.6 0.0 copy-start
  0.7 0.8 broadcast_select_fusion.1
  1.5 0.2 convert_reduce_fusion.1
  1.7 0.2 fusion.4
  1.9 0.2 select_reduce_fusion
  2.0 0.1 convert_reduce_fusion
  2.1 0.1 fusion.2
  2.2 0.7 fusion.10
  2.9 0.1 concatenate.3.table
  3.0 1.1 fusion.12
  4.0 0.1 copy.35
  4.2 1.4 %fusion.1.msg0 = bf16[32,32,128]{2,1,0:T(8,128)(2,1)S(1)} fusion(f32[32,32,1,128]{3,2,1,0:T(1,128)} %param.9, bf16[1,32,32,1,128]{4,2,3,1,0:T(8,128)(2,1)S(1)} %get-tuple-element.26), kind=kLoop, calls=%fused_computation.3 | loop fusion | flops 393216 | bytes 1048576 | tf_op jit(solution)/shard_map/transpose | solution.py:273
  5.6 0.0 copy-done.1
  5.6 0.2 copy.34
  5.8 0.0 copy-done
  5.8 115.6 %shard_map.85 = (bf16[64,128,128]{2,1,0:T(8,128)(2,1)S(1)}, f32[32,32,128]{2,1,0:T(8,128)S(1)}, f32[64,128]{1,0:T(8,128)S(1)}) custom-call(s32[640]{0:T(1024)S(1)} %concatenate.3.table, bf16[64,128,128]{2,1,0:T(8,128)(2,1)S(1)} %copy-done, bf16[32,32,128]{2,1,0:T(8,128)(2,1)S(1)} %fusion.1.msg0, bf16[32,32,128]{2,1,0:T(8,128)(2,1)S(1)} %bitcast.27, ...), custom_call_target="tpu_custom_call" | custom-call | tf_op jit(solution)/shard_map/pallas_call | solution.py:284
  121.5 0.1 slice_reduce_fusion.1
  121.6 0.6 maximum_log_fusion
  122.2 1.3 %copy.23 = f32[32,32,1,128]{3,2,1,0:T(1,128)} copy(f32[32,32,1,128]{3,0,1,2:T(8,128)S(1)} %bitcast.28) | data formatting | bytes 1048576
  123.5 1.3 %copy.37 = bf16[64,128,128]{2,1,0:T(8,128)(2,1)} copy(bf16[64,128,128]{2,1,0:T(8,128)(2,1)S(1)} %get-tuple-element.31) | data formatting | bytes 4194304
  (4 shorter events, 0.0 us)
Async XLA Ops:
  0.6 5.0 %copy-start.1 = (bf16[2,32,32,1,128]{4,2,3,1,0:T(8,128)(2,1)S(1)}, bf16[2,32,32,1,128]{4,2,3,1,0:T(8,128)(2,1)}, u32[]{:S(2)}) copy-start(bf16[2,32,32,1,128]{4,2,3,1,0:T(8,128)(2,1)} %param.11) | copy-start | bytes 1572868
  0.6 5.2 %copy-start = (bf16[64,128,128]{2,1,0:T(8,128)(2,1)S(1)}, bf16[64,128,128]{2,1,0:T(8,128)(2,1)}, u32[]{:S(2)}) copy-start(bf16[64,128,128]{2,1,0:T(8,128)(2,1)} %trans.1) | copy-start | bytes 6291460
where the time goes:
time: 125 us
  Pallas kernels  116 us (93%)
  other arithmetic  4.25 us (3%)
  local copies, waits for them, and re-layouts  4.22 us (3%)
    pallas_call x1, Pallas kernels, body(): pl.pallas_call(functools.partial(kernel, nd, ns, float(total_states)), ou...  116 us
    unnamed x8, local copies, waits for them, and re-layouts  2.97 us

commit v1 on v0

--- a/solution.py
+++ b/solution.py
@@ -11,10 +11,11 @@
 
 
 def kernel(nd, ns, total_states, table,
-           trans, msg0, em1, fwd, counts, beta, scales,
-           msgs0, msgs1, fwds0, fwds1, run, parts, ypart, zsend, zpart, tdst, tsrc,
+           last_in, trans, msg0, em1, fwd, counts, beta, scales,
+           msgs0, msgs1, fwds0, fwds1, prods0, prods1, runs0, runs1,
+           mates0, mates1, last_mate, last_table, zsend, zpart, tdst, tsrc,
            send_m, recv_m, send_f, recv_f, send_y, recv_y, send_z, recv_z,
-           send_td, recv_td, send_ts, recv_ts):
+           send_td, recv_td, send_ts, recv_ts, send_l, recv_l, local_l):
     local, seqs, blk = msg0.shape
     slots = trans.shape[0]
     nz, nx = nd // 2, ns // 2
@@ -41,6 +42,9 @@
     pl.semaphore_wait(barrier, nd + ns - 2)
 
     msgs, fwds = (msgs0, msgs1), (fwds0, fwds1)
+    prods, runs, mates = (prods0, prods1), (runs0, runs1), (mates0, mates1)
+    chunks = send_y.shape[1]
+    part = slots // chunks
     pending = []
 
     def other(pos, o):
@@ -91,49 +95,48 @@
     def forward_pass(k, offsets):
         gather_pass(fwds, k, me_d, offsets, nz, mate_d, send_f, recv_f)
 
+    def rows_of(k, chunk):
+        piece = pl.ds(1 + chunk * part, part)
+        return copy(runs[k].at[piece], mates[k].at[piece], send_y.at[k, chunk],
+                    recv_y.at[k, chunk], mate_d)
+
     def products(k):
-        run[0] = jnp.zeros((seqs, blk), jnp.float32)
-
-        def one(j, carry):
-            c = table[slots + j]
-            block = msgs[k][c // local, c % local]
-            run[j + 1] = lax.dot_general(block, trans[table[j]], (((1,), (1,)), ((), ())),
-                                         preferred_element_type=jnp.float32)
-            return carry
-
-        lax.fori_loop(0, slots, one, 0, unroll=8)
-
-        def add_run(j, acc):
-            acc = run[j + 1] + acc * table[2 * slots + j].astype(jnp.float32)
-            run[j + 1] = acc
-            return acc
-
-        lax.fori_loop(0, slots, add_run, jnp.zeros((seqs, blk), jnp.float32), unroll=4)
-
-        for d in range(nd):
-            def put(a, carry, d=d):
-                parts[k, d, a] = run[table[6 * slots + d * local + a]].astype(jnp.bfloat16)
+        acc = jnp.zeros((seqs, blk), jnp.float32)
+        runs[k][0] = acc.astype(jnp.bfloat16)
+        mates[k][0] = acc.astype(jnp.bfloat16)
+        for chunk in range(chunks):
+            def one(j, carry):
+                c = table[slots + j]
+                prods[k][j] = lax.dot_general(
+                    msgs[k][c // local, c % local], trans[table[j]], (((1,), (1,)), ((), ())),
+                    preferred_element_type=jnp.float32)
                 return carry
 
-            lax.fori_loop(0, local, put, 0, unroll=4)
-
-    def reduce_side(k):
-        for o in reversed(range(nz)):
-            zt = other(z, o)
-            c = copy(parts.at[k, zt * 2 + 1 - y], ypart.at[k, zt], send_y.at[k, o],
-                     recv_y.at[k, zt], mate_d)
+            def add_run(j, acc):
+                acc = prods[k][j] + acc * table[2 * slots + j].astype(jnp.float32)
+                runs[k][j + 1] = acc.astype(jnp.bfloat16)
+                return acc
+
+            lax.fori_loop(chunk * part, (chunk + 1) * part, one, 0, unroll=8)
+            acc = lax.fori_loop(chunk * part, (chunk + 1) * part, add_run, acc, unroll=4)
+            c = rows_of(k, chunk)
             c.start()
             pending.append(c)
 
+    def two_rows(k, d, a):
+        r = d * local + a
+        own = runs[k][table[8 * slots + r]]
+        mate = mates[k][last_table[r // 128, r % 128]]
+        return own.astype(jnp.float32) + mate.astype(jnp.float32)
+
     def reduce_line(k):
+        for chunk in range(chunks):
+            rows_of(k, chunk).wait_recv()
         for o in reversed(range(1, nz)):
             zt = other(z, o)
-            copy(parts.at[k, zt * 2 + 1 - y], ypart.at[k, zt], send_y.at[k, o],
-                 recv_y.at[k, zt], mate_d).wait_recv()
 
             def add(a, carry):
-                zsend[k, zt, a] = (parts[k, zt * 2 + y, a].astype(jnp.float32)
-                                   + ypart[k, zt, a].astype(jnp.float32)).astype(jnp.bfloat16)
+                zsend[k, zt, a] = two_rows(k, zt * 2 + y, a).astype(jnp.bfloat16)
                 return carry
 
             lax.fori_loop(0, local, add, 0, unroll=4)
@@ -142,25 +145,29 @@
             c.start()
             pending.append(c)
 
-    def reduce_end(k):
-        copy(parts.at[k, z * 2 + 1 - y], ypart.at[k, z], send_y.at[k, 0],
-             recv_y.at[k, z], mate_d).wait_recv()
+    def reduce_end(k, use):
         for o in range(1, nz):
             zf = other(z, o)
             copy(zsend.at[k, zf], zpart.at[k, zf], send_z.at[k, o - 1], recv_z.at[k, zf],
                  mate_d).wait_recv()
 
-        def add(a, total):
-            raw = parts[k, me_d, a].astype(jnp.float32) + ypart[k, z, a].astype(jnp.float32)
+        def add(a, carry):
+            raw = two_rows(k, me_d, a)
             for o in range(1, nz):
                 raw = raw + zpart[k, other(z, o), a].astype(jnp.float32)
-            beta[a] = raw
-            if k == 0:
-                msgs[1][me_s, a] = (em1[a].astype(jnp.float32) * raw).astype(jnp.bfloat16)
-            return total + fwd[k, a].astype(jnp.float32) * raw
-
-        total = lax.fori_loop(0, local, add, jnp.zeros((seqs, blk), jnp.float32), unroll=2)
-        tdst[me_d, pl.ds(k * seqs, seqs)] = total
+            use(a, raw)
+            return carry
+
+        lax.fori_loop(0, local, add, 0, unroll=2)
+
+    def terms(k):
+        def term(j, total):
+            r = table[6 * slots + j]
+            value = prods[k][j] * fwds[k][r // local, r % local].astype(jnp.float32)
+            return total + value * table[7 * slots + j].astype(jnp.float32)
+
+        tdst[me_d, pl.ds(k * seqs, seqs)] = lax.fori_loop(
+            0, slots, term, jnp.zeros((seqs, blk), jnp.float32), unroll=4)
 
     def keep_message(a, carry):
         msgs[0][me_s, a] = msg0[a]
@@ -168,6 +175,9 @@
 
     lax.fori_loop(0, local, keep_message, 0, unroll=4)
     message_gather(0)
+    last_copy = copy(last_in, last_mate, send_l, recv_l, mate_d)
+    last_copy.start()
+    pending.append(last_copy)
     for k in range(2):
         def keep_forward(a, carry, k=k):
             fwds[k][me_d, a] = fwd[k, a]
@@ -176,24 +186,32 @@
         lax.fori_loop(0, local, keep_forward, 0, unroll=4)
     gather_line(fwds, 0, me_d, nz, at_dst, send_f, recv_f)
     gather_side(fwds, 0, me_d, mate_d, send_f, recv_f)
+    last_copy.wait_recv()
+    to_table = pltpu.make_async_copy(last_mate, last_table, local_l)
+    to_table.start()
+    to_table.wait()
     message_arrive(0)
     forward_pass(0, range(1, 2))
     products(0)
-    reduce_side(0)
     reduce_line(0)
     forward_pass(0, range(2, nz))
     gather_side(fwds, 1, me_d, mate_d, send_f, recv_f)
+
+    def next_message(a, raw):
+        msgs[1][me_s, a] = (em1[a].astype(jnp.float32) * raw).astype(jnp.bfloat16)
+
+    reduce_end(0, next_message)
+
+    message_gather(1)
     gather_line(fwds, 1, me_d, nz, at_dst, send_f, recv_f)
-    reduce_end(0)
-
-    message_gather(1)
     message_arrive(1)
     forward_pass(1, range(1, 2))
     products(1)
-    reduce_side(1)
     reduce_line(1)
     forward_pass(1, range(2, nz))
-    reduce_end(1)
+    for k in range(2):
+        gather_end(fwds, k, me_d, nz, mate_d, send_f, recv_f)
+        terms(k)
 
     for o in range(1, nd):
         c = copy(tdst.at[me_d], tdst.at[me_d], send_td.at[o - 1], recv_td.at[me_d],
@@ -218,15 +236,6 @@
     scales[...] = norm
     inverse = 1.0 / norm
 
-    def finish(a, carry):
-        beta[a] = beta[a] / norm[seqs:]
-        return carry
-
-    lax.fori_loop(0, local, finish, 0)
-
-    for k in range(2):
-        gather_end(fwds, k, me_d, nz, mate_d, send_f, recv_f)
-
     def count(m, carry):
         r, c = table[3 * slots + m], table[4 * slots + m]
         left = jnp.concatenate([fwds[k][r // local, r % local] for k in range(2)], axis=0)
@@ -238,6 +247,11 @@
         return carry
 
     lax.fori_loop(0, slots, count, 0, unroll=4)
+
+    def last_beta(a, raw):
+        beta[a] = raw * inverse[seqs:]
+
+    reduce_end(1, last_beta)
     for c in pending:
         c.wait_send()
 
@@ -263,11 +277,16 @@
     same = jnp.any((key[None, :] == key[:, None]) & (rank[None, :] == rank[:, None] - 1), axis=1)
     flag = jnp.sum(place * same[None, :].astype(jnp.int32), axis=1)
     every = jnp.arange(rows)
+    prow = jnp.sum(place * row[None, :], axis=1)
+    plive = jnp.sum(place * live[None, :].astype(jnp.int32), axis=1)
     last = jnp.where(jnp.any(key[None, :] == every[:, None], axis=1),
                      jnp.sum((key[None, :] <= every[:, None]).astype(jnp.int32), axis=1), 0)
 
     table = jnp.concatenate(
-        [perm, pcol, flag, row, col, live.astype(jnp.int32), last]).astype(jnp.int32)
+        [perm, pcol, flag, row, col, live.astype(jnp.int32), prow, plive, last]).astype(jnp.int32)
+
+    lines = -(-rows // 128)
+    last2 = jnp.pad(last.astype(jnp.int32), (0, lines * 128 - rows)).reshape(lines, 128)
 
     def by_block(array):
         return jnp.swapaxes(array[..., 0, :], -3, -2)
@@ -288,30 +307,36 @@
             jax.ShapeDtypeStruct(block, jnp.float32),
             jax.ShapeDtypeStruct((2 * seqs, blk), jnp.float32),
         ),
-        in_specs=[smem] + [vmem] * 4,
+        in_specs=[smem] + [vmem] * 5,
         out_specs=(vmem, vmem, vmem),
         scratch_shapes=[
             pltpu.VMEM((ns,) + block, jnp.bfloat16),
             pltpu.VMEM((ns,) + block, jnp.bfloat16),
             pltpu.VMEM((nd,) + block, jnp.bfloat16),
             pltpu.VMEM((nd,) + block, jnp.bfloat16),
-            pltpu.VMEM((slots + 1, seqs, blk), jnp.float32),
-            pltpu.VMEM((2, nd) + block, jnp.bfloat16),
-            pltpu.VMEM((2, nz) + block, jnp.bfloat16),
+            pltpu.VMEM((slots, seqs, blk), jnp.float32),
+            pltpu.VMEM((slots, seqs, blk), jnp.float32),
+            pltpu.VMEM((slots + 1, seqs, blk), jnp.bfloat16),
+            pltpu.VMEM((slots + 1, seqs, blk), jnp.bfloat16),
+            pltpu.VMEM((slots + 1, seqs, blk), jnp.bfloat16),
+            pltpu.VMEM((slots + 1, seqs, blk), jnp.bfloat16),
+            pltpu.VMEM((lines, 128), jnp.int32),
+            pltpu.SMEM((lines, 128), jnp.int32),
             pltpu.VMEM((2, nz) + block, jnp.bfloat16),
             pltpu.VMEM((2, nz) + block, jnp.bfloat16),
             pltpu.VMEM((nd, 2 * seqs, blk), jnp.float32),
             pltpu.VMEM((ns, 2 * seqs, blk), jnp.float32),
             dma((2, 2 * nx)), dma((2, ns)),
             dma((2, 2 * nz)), dma((2, nd)),
-            dma((2, nz)), dma((2, nz)),
+            dma((2, 4)), dma((2, 4)),
             dma((2, nz)), dma((2, nz)),
             dma((nd,)), dma((nd,)),
             dma((ns,)), dma((ns,)),
+            dma, dma, dma,
         ],
         compiler_params=pltpu.CompilerParams(
             collective_id=0, has_side_effects=True, vmem_limit_bytes=48 * 1024 * 1024),
-    )(table, transitions, msg0, em1, fwd)
+    )(table, last2, transitions, msg0, em1, fwd)
     first, second = scales[:seqs, 0], scales[seqs:, 0]
     logs = jnp.log(jnp.stack([first, second / first]))
     return counts, jnp.swapaxes(beta, 0, 1)[:, :, None, :], logs

time: 125 us -> 129 us (1.032)
  Pallas kernels: 116 us -> 119 us
    pallas_call x1, Pallas kernels: 116 us -> 119 us  [body(): pl.pallas_call(functools.partial(kernel, nd, ns, float(total_states)), ou...]
where the time goes in v1:
time: 129 us; the launch traced here: 128 us
  Pallas kernels  119 us (92%)
  other arithmetic  4.28 us (3%)
  local copies, waits for them, and re-layouts  4.23 us (3%)
    pallas_call x1, Pallas kernels, body(): pl.pallas_call(functools.partial(kernel, nd, ns, float(total_states)), ou...  119 us
    unnamed x8, local copies, waits for them, and re-layouts  2.97 us

profile of v1, /device:TPU:0, one launch (start us, length us, event | category | flops | bytes accessed | tf_op | source)
XLA Modules:
  0.0 127.9 jit_solution(11287927628234021185)
XLA Ops:
  0.6 0.0 copy-start.1
  0.6 0.0 copy-start
  0.7 0.8 broadcast_select_fusion.1
  1.5 0.2 convert_reduce_fusion.1
  1.7 0.2 fusion.4
  1.9 0.7 fusion.10
  2.5 0.2 select_reduce_fusion
  2.7 0.1 convert_reduce_fusion
  2.8 0.1 fusion.2
  2.9 0.1 concatenate.3.table
  3.0 1.1 fusion.12
  4.1 0.1 copy.35
  4.2 1.4 %fusion.1.msg0 = bf16[32,32,128]{2,1,0:T(8,128)(2,1)S(1)} fusion(f32[32,32,1,128]{3,2,1,0:T(1,128)} %param.9, bf16[1,32,32,1,128]{4,2,3,1,0:T(8,128)(2,1)S(1)} %get-tuple-element.28), kind=kLoop, calls=%fused_computation.3 | loop fusion | flops 393216 | bytes 1048576 | tf_op jit(solution)/shard_map/transpose | solution.py:292
  5.6 0.0 copy-done.1
  5.6 0.2 copy.34
  5.8 0.0 copy-done
  5.9 118.7 %shard_map.85 = (bf16[64,128,128]{2,1,0:T(8,128)(2,1)S(1)}, f32[32,32,128]{2,1,0:T(8,128)S(1)}, f32[64,128]{1,0:T(8,128)S(1)}) custom-call(s32[768]{0:T(1024)S(1)} %concatenate.3.table, s32[2,128]{1,0:T(2,128)S(1)} %bitcast.30, bf16[64,128,128]{2,1,0:T(8,128)(2,1)S(1)} %copy-done, bf16[32,32,128]{2,1,0:T(8,128)(2,1)S(1)} %fusion.1.msg0, ...), custom_call_target="tpu_custom_call" | custom-call | tf_op jit(solution)/shard_map/pallas_call | solution.py:303
  124.6 0.1 slice_reduce_fusion.1
  124.7 0.6 maximum_log_fusion
  125.3 1.3 %copy.23 = f32[32,32,1,128]{3,2,1,0:T(1,128)} copy(f32[32,32,1,128]{3,0,1,2:T(8,128)S(1)} %bitcast.29) | data formatting | bytes 1048576
  126.6 1.3 %copy.37 = bf16[64,128,128]{2,1,0:T(8,128)(2,1)} copy(bf16[64,128,128]{2,1,0:T(8,128)(2,1)S(1)} %get-tuple-element.33) | data formatting | bytes 4194304
  (4 shorter events, 0.0 us)
Async XLA Ops:
  0.6 5.0 %copy-start.1 = (bf16[2,32,32,1,128]{4,2,3,1,0:T(8,128)(2,1)S(1)}, bf16[2,32,32,1,128]{4,2,3,1,0:T(8,128)(2,1)}, u32[]{:S(2)}) copy-start(bf16[2,32,32,1,128]{4,2,3,1,0:T(8,128)(2,1)} %param.11) | copy-start | bytes 1572868
  0.6 5.2 %copy-start = (bf16[64,128,128]{2,1,0:T(8,128)(2,1)S(1)}, bf16[64,128,128]{2,1,0:T(8,128)(2,1)}, u32[]{:S(2)}) copy-start(bf16[64,128,128]{2,1,0:T(8,128)(2,1)} %trans.1) | copy-start | bytes 6291460

commit v2 on v1

--- a/solution.py
+++ b/solution.py
@@ -15,7 +15,7 @@
            msgs0, msgs1, fwds0, fwds1, prods0, prods1, runs0, runs1,
            mates0, mates1, last_mate, last_table, zsend, zpart, tdst, tsrc,
            send_m, recv_m, send_f, recv_f, send_y, recv_y, send_z, recv_z,
-           send_td, recv_td, send_ts, recv_ts, send_l, recv_l, local_l):
+           send_td, recv_td, send_ts, recv_ts, send_l, recv_l, local_l, send_p, send_r):
     local, seqs, blk = msg0.shape
     slots = trans.shape[0]
     nz, nx = nd // 2, ns // 2
@@ -45,7 +45,8 @@
     prods, runs, mates = (prods0, prods1), (runs0, runs1), (mates0, mates1)
     chunks = send_y.shape[1]
     part = slots // chunks
-    pending = []
+    pending, guards = [], []
+    first_way = 1 - z // (nz // 2)
 
     def other(pos, o):
         for bit in range(o.bit_length()):
@@ -92,8 +93,33 @@
         gather_pass(msgs, k, me_s, range(1, nx), nx, mate_s, send_m, recv_m)
         gather_end(msgs, k, me_s, nx, mate_s, send_m, recv_m)
 
-    def forward_pass(k, offsets):
-        gather_pass(fwds, k, me_d, offsets, nz, mate_d, send_f, recv_f)
+    def guarded(cond, make):
+        pl.when(cond)(lambda: make().start())
+        guards.append((cond, make))
+
+    def forward_line(k):
+        def to(step):
+            return lambda: copy(fwds[k].at[me_d], fwds[k].at[me_d], send_f.at[k, 1 + step],
+                                recv_f.at[k, me_d], at_dst((z - 1 + 2 * step) * 2 + y))
+
+        guarded(z < nz - 1, to(1))
+        guarded(z > 0, to(0))
+
+    def forward_hop(k, h):
+        for sign, there, more in ((-1, z >= h, z < nz - 1), (1, z + h <= nz - 1, z > 0)):
+            e = (z + sign * h) * 2 + y
+            block = fwds[k].at[e]
+
+            def relay(e=e, block=block, sign=sign):
+                return copy(block, block, send_r.at[k, e], recv_f.at[k, e],
+                            at_dst((z - sign) * 2 + y))
+
+            def across(e=e, block=block):
+                return copy(block, block, send_p.at[k, e], recv_f.at[k, e], mate_d)
+
+            pl.when(there)(lambda across=across: across().wait_recv())
+            guarded(there & more, relay)
+            guarded(there, across)
 
     def rows_of(k, chunk):
         piece = pl.ds(1 + chunk * part, part)
@@ -132,33 +158,58 @@
     def reduce_line(k):
         for chunk in range(chunks):
             rows_of(k, chunk).wait_recv()
-        for o in reversed(range(1, nz)):
-            zt = other(z, o)
-
-            def add(a, carry):
-                zsend[k, zt, a] = two_rows(k, zt * 2 + y, a).astype(jnp.bfloat16)
-                return carry
-
-            lax.fori_loop(0, local, add, 0, unroll=4)
-            c = copy(zsend.at[k, zt], zpart.at[k, z], send_z.at[k, o - 1], recv_z.at[k, z],
-                     at_dst(zt * 2 + y))
-            c.start()
-            pending.append(c)
+        for turn in range(2):
+            way = first_way if turn == 0 else 1 - first_way
+            step = 2 * way - 1
+            count = way * (nz - 1 - z) + (1 - way) * z
+            before = z * way + (nz - 1 - z) * (1 - way)
+            for q in reversed(range(1, nz)):
+                zt = z + step * q
+
+                def send(zt=zt, way=way, step=step):
+                    return copy(zsend.at[k, zt], zpart.at[k, way, zt], send_z.at[k, zt],
+                                recv_z.at[k, way, zt], at_dst((z + step) * 2 + y))
+
+                def work(zt=zt, way=way, send=send):
+                    def add(a, carry):
+                        zsend[k, zt, a] = (two_rows(k, zt * 2 + y, a)
+                                           + zpart[k, way, zt, a].astype(jnp.float32)
+                                           ).astype(jnp.bfloat16)
+                        return carry
+
+                    lax.fori_loop(0, local, add, 0, unroll=4)
+                    send().start()
+
+                pl.when((q <= count) & (before > 0))(lambda send=send: send().wait_recv())
+                pl.when(q <= count)(work)
+                guards.append((q <= count, send))
 
     def reduce_end(k, use):
-        for o in range(1, nz):
-            zf = other(z, o)
-            copy(zsend.at[k, zf], zpart.at[k, zf], send_z.at[k, o - 1], recv_z.at[k, zf],
-                 mate_d).wait_recv()
+        def arrived(way):
+            return lambda: copy(zsend.at[k, z], zpart.at[k, way, z], send_z.at[k, z],
+                                recv_z.at[k, way, z], mate_d).wait_recv()
+
+        pl.when(z > 0)(arrived(1))
+        pl.when(z < nz - 1)(arrived(0))
 
         def add(a, carry):
-            raw = two_rows(k, me_d, a)
-            for o in range(1, nz):
-                raw = raw + zpart[k, other(z, o), a].astype(jnp.float32)
+            raw = (two_rows(k, me_d, a) + zpart[k, 0, z, a].astype(jnp.float32)
+                   + zpart[k, 1, z, a].astype(jnp.float32))
             use(a, raw)
             return carry
 
         lax.fori_loop(0, local, add, 0, unroll=2)
+
+    def clear(way):
+        def run():
+            def one(a, carry):
+                for k in range(2):
+                    for zt in range(nz):
+                        zpart[k, way, zt, a] = jnp.zeros((seqs, blk), jnp.bfloat16)
+                return carry
+
+            lax.fori_loop(0, local, one, 0)
+        return run
 
     def terms(k):
         def term(j, total):
@@ -184,17 +235,20 @@
             return carry
 
         lax.fori_loop(0, local, keep_forward, 0, unroll=4)
-    gather_line(fwds, 0, me_d, nz, at_dst, send_f, recv_f)
+    forward_line(0)
     gather_side(fwds, 0, me_d, mate_d, send_f, recv_f)
     last_copy.wait_recv()
     to_table = pltpu.make_async_copy(last_mate, last_table, local_l)
     to_table.start()
     to_table.wait()
+    pl.when(z == 0)(clear(1))
+    pl.when(z == nz - 1)(clear(0))
     message_arrive(0)
-    forward_pass(0, range(1, 2))
+    forward_hop(0, 1)
     products(0)
     reduce_line(0)
-    forward_pass(0, range(2, nz))
+    for h in range(2, nz):
+        forward_hop(0, h)
     gather_side(fwds, 1, me_d, mate_d, send_f, recv_f)
 
     def next_message(a, raw):
@@ -203,12 +257,13 @@
     reduce_end(0, next_message)
 
     message_gather(1)
-    gather_line(fwds, 1, me_d, nz, at_dst, send_f, recv_f)
+    forward_line(1)
     message_arrive(1)
-    forward_pass(1, range(1, 2))
+    forward_hop(1, 1)
     products(1)
     reduce_line(1)
-    forward_pass(1, range(2, nz))
+    for h in range(2, nz):
+        forward_hop(1, h)
     for k in range(2):
         gather_end(fwds, k, me_d, nz, mate_d, send_f, recv_f)
         terms(k)
@@ -254,6 +309,8 @@
     reduce_end(1, last_beta)
     for c in pending:
         c.wait_send()
+    for cond, make in guards:
+        pl.when(cond)(lambda make=make: make().wait_send())
 
 
 def body(nd, ns, transitions, row_block, col_block, beta_last, emissions, forward):
@@ -323,16 +380,16 @@
             pltpu.VMEM((lines, 128), jnp.int32),
             pltpu.SMEM((lines, 128), jnp.int32),
             pltpu.VMEM((2, nz) + block, jnp.bfloat16),
-            pltpu.VMEM((2, nz) + block, jnp.bfloat16),
+            pltpu.VMEM((2, 2, nz) + block, jnp.bfloat16),
             pltpu.VMEM((nd, 2 * seqs, blk), jnp.float32),
             pltpu.VMEM((ns, 2 * seqs, blk), jnp.float32),
             dma((2, 2 * nx)), dma((2, ns)),
-            dma((2, 2 * nz)), dma((2, nd)),
+            dma((2, 3)), dma((2, nd)),
             dma((2, 4)), dma((2, 4)),
-            dma((2, nz)), dma((2, nz)),
+            dma((2, nz)), dma((2, 2, nz)),
             dma((nd,)), dma((nd,)),
             dma((ns,)), dma((ns,)),
-            dma, dma, dma,
+            dma, dma, dma, dma((2, nd)), dma((2, nd)),
         ],
         compiler_params=pltpu.CompilerParams(
             collective_id=0, has_side_effects=True, vmem_limit_bytes=48 * 1024 * 1024),

time: 129 us -> 147 us (1.14)
  Pallas kernels: 119 us -> 138 us
    pallas_call x1, Pallas kernels: 119 us -> 138 us  [body(): pl.pallas_call(functools.partial(kernel, nd, ns, float(total_states)), ou...]
where the time goes in v2:
time: 147 us
  Pallas kernels  138 us (94%)
  other arithmetic  4.28 us (3%)
  local copies, waits for them, and re-layouts  4.23 us (3%)
    pallas_call x1, Pallas kernels, body(): pl.pallas_call(functools.partial(kernel, nd, ns, float(total_states)), ou...  138 us
    unnamed x8, local copies, waits for them, and re-layouts  2.97 us

profile of v2, /device:TPU:0, one launch (start us, length us, event | category | flops | bytes accessed | tf_op | source)
XLA Modules:
  0.0 147.2 jit_solution(9305865148043942744)
XLA Ops:
  0.6 0.0 copy-start.1
  0.6 0.0 copy-start
  0.7 0.8 broadcast_select_fusion.1
  1.5 0.2 convert_reduce_fusion.1
  1.7 0.2 fusion.4
  1.9 0.7 fusion.10
  2.5 0.2 select_reduce_fusion
  2.7 0.1 convert_reduce_fusion
  2.8 0.1 fusion.2
  2.9 0.1 concatenate.3.table
  3.0 1.1 fusion.12
  4.1 0.1 copy.35
  4.2 1.4 fusion.1.msg0
  5.6 0.0 copy-done.1
  5.6 0.2 copy.34
  5.8 0.0 copy-done
  5.9 137.9 %shard_map.85 = (bf16[64,128,128]{2,1,0:T(8,128)(2,1)S(1)}, f32[32,32,128]{2,1,0:T(8,128)S(1)}, f32[64,128]{1,0:T(8,128)S(1)}) custom-call(s32[768]{0:T(1024)S(1)} %concatenate.3.table, s32[2,128]{1,0:T(2,128)S(1)} %bitcast.30, bf16[64,128,128]{2,1,0:T(8,128)(2,1)S(1)} %copy-done, bf16[32,32,128]{2,1,0:T(8,128)(2,1)S(1)} %fusion.1.msg0, ...), custom_call_target="tpu_custom_call" | custom-call | tf_op jit(solution)/shard_map/pallas_call | solution.py:360
  143.8 0.1 slice_reduce_fusion.1
  143.9 0.6 maximum_log_fusion
  144.5 1.3 copy.23
  145.8 1.3 copy.37
  (4 shorter events, 0.0 us)
Async XLA Ops:
  0.6 5.0 %copy-start.1 = (bf16[2,32,32,1,128]{4,2,3,1,0:T(8,128)(2,1)S(1)}, bf16[2,32,32,1,128]{4,2,3,1,0:T(8,128)(2,1)}, u32[]{:S(2)}) copy-start(bf16[2,32,32,1,128]{4,2,3,1,0:T(8,128)(2,1)} %param.11) | copy-start | bytes 1572868
  0.6 5.2 %copy-start = (bf16[64,128,128]{2,1,0:T(8,128)(2,1)S(1)}, bf16[64,128,128]{2,1,0:T(8,128)(2,1)}, u32[]{:S(2)}) copy-start(bf16[64,128,128]{2,1,0:T(8,128)(2,1)} %trans.1) | copy-start | bytes 6291460

commit v3 on v0

--- a/solution.py
+++ b/solution.py
@@ -11,11 +11,11 @@
 
 
 def kernel(nd, ns, total_states, table,
-           trans, msg0, em1, fwd, counts, beta, scales,
+           trans, beta_in, emitted, fwd, counts, beta, scales,
            msgs0, msgs1, fwds0, fwds1, run, parts, ypart, zsend, zpart, tdst, tsrc,
            send_m, recv_m, send_f, recv_f, send_y, recv_y, send_z, recv_z,
            send_td, recv_td, send_ts, recv_ts):
-    local, seqs, blk = msg0.shape
+    local, seqs, blk = beta_in.shape
     slots = trans.shape[0]
     nz, nx = nd // 2, ns // 2
     me_d, me_s = lax.axis_index("dst"), lax.axis_index("src")
@@ -110,12 +110,11 @@
 
         lax.fori_loop(0, slots, add_run, jnp.zeros((seqs, blk), jnp.float32), unroll=4)
 
-        for d in range(nd):
-            def put(a, carry, d=d):
-                parts[k, d, a] = run[table[6 * slots + d * local + a]].astype(jnp.bfloat16)
-                return carry
-
-            lax.fori_loop(0, local, put, 0, unroll=4)
+        def put(r, carry):
+            parts[k, r // local, r % local] = run[table[6 * slots + r]].astype(jnp.bfloat16)
+            return carry
+
+        lax.fori_loop(0, nd * local, put, 0, unroll=8)
 
     def reduce_side(k):
         for o in reversed(range(nz)):
@@ -156,14 +155,14 @@
                 raw = raw + zpart[k, other(z, o), a].astype(jnp.float32)
             beta[a] = raw
             if k == 0:
-                msgs[1][me_s, a] = (em1[a].astype(jnp.float32) * raw).astype(jnp.bfloat16)
+                msgs[1][me_s, a] = (emitted[1, a].astype(jnp.float32) * raw).astype(jnp.bfloat16)
             return total + fwd[k, a].astype(jnp.float32) * raw
 
         total = lax.fori_loop(0, local, add, jnp.zeros((seqs, blk), jnp.float32), unroll=2)
         tdst[me_d, pl.ds(k * seqs, seqs)] = total
 
     def keep_message(a, carry):
-        msgs[0][me_s, a] = msg0[a]
+        msgs[0][me_s, a] = (emitted[0, a].astype(jnp.float32) * beta_in[a]).astype(jnp.bfloat16)
         return carry
 
     lax.fori_loop(0, local, keep_message, 0, unroll=4)
@@ -272,8 +271,8 @@
     def by_block(array):
         return jnp.swapaxes(array[..., 0, :], -3, -2)
 
-    msg0 = by_block((emissions[0].astype(jnp.float32) * beta_last).astype(jnp.bfloat16))
-    em1 = by_block(emissions[1])
+    beta_in = by_block(beta_last)
+    emitted = by_block(emissions)
     fwd = by_block(forward)
 
     smem = pl.BlockSpec(memory_space=pltpu.SMEM)
@@ -311,7 +310,7 @@
         ],
         compiler_params=pltpu.CompilerParams(
             collective_id=0, has_side_effects=True, vmem_limit_bytes=48 * 1024 * 1024),
-    )(table, transitions, msg0, em1, fwd)
+    )(table, transitions, beta_in, emitted, fwd)
     first, second = scales[:seqs, 0], scales[seqs:, 0]
     logs = jnp.log(jnp.stack([first, second / first]))
     return counts, jnp.swapaxes(beta, 0, 1)[:, :, None, :], logs

time: 125 us -> 125 us (level)
  other arithmetic: 4.25 us -> 2.73 us
    transpose x0 -> x1, local copies, waits for them, and re-layouts: none -> 1.61 us  [by_block(): return jnp.swapaxes(array[..., 0, :], -3, -2)]
    transpose x1 -> x0, other arithmetic: 1.43 us -> none  [by_block(): return jnp.swapaxes(array[..., 0, :], -3, -2)]
    unnamed x8 -> x5, local copies, waits for them, and re-layouts: 2.97 us -> 2.96 us
where the time goes in v3:
time: 125 us
  Pallas kernels  117 us (94%)
  local copies, waits for them, and re-layouts  4.76 us (4%)
  other arithmetic  2.73 us (2%)
    pallas_call x1, Pallas kernels, body(): pl.pallas_call(functools.partial(kernel, nd, ns, float(total_states)), ou...  117 us
    unnamed x5, local copies, waits for them, and re-layouts  2.96 us

profile of v3, /device:TPU:0, one launch (start us, length us, event | category | flops | bytes accessed | tf_op | source)
XLA Modules:
  0.0 124.9 jit_solution(12023060339722890091)
XLA Ops:
  0.6 0.0 copy-start
  0.6 0.8 broadcast_select_fusion.1
  1.4 0.2 convert_reduce_fusion.1
  1.6 0.2 fusion.2
  1.8 0.2 select_reduce_fusion
  1.9 0.1 convert_reduce_fusion
  2.0 0.1 fusion
  2.1 0.7 fusion.8
  2.8 0.1 concatenate.3.table
  2.9 1.6 %copy_bitcast_fusion = (bf16[2,32,32,128]{3,2,1,0:T(8,128)(2,1)S(1)}, bf16[2,32,32,128]{3,2,1,0:T(8,128)(2,1)S(1)}) fusion(bf16[2,32,32,1,128]{4,2,3,1,0:T(8,128)(2,1)} %param.11, bf16[2,32,32,1,128]{4,2,3,1,0:T(8,128)(2,1)} %param.10), kind=kLoop, calls=%fused_computation | loop fusion | bytes 2097152 | tf_op jit(solution)/shard_map/transpose | solution.py:272
  4.5 0.0 copy-done
  4.5 0.3 copy.24
  4.8 116.7 %shard_map.85 = (bf16[64,128,128]{2,1,0:T(8,128)(2,1)S(1)}, f32[32,32,128]{2,1,0:T(8,128)S(1)}, f32[64,128]{1,0:T(8,128)S(1)}) custom-call(s32[640]{0:T(1024)S(1)} %concatenate.3.table, bf16[64,128,128]{2,1,0:T(8,128)(2,1)} %trans.1, f32[32,32,128]{2,1,0:T(8,128)S(1)} %bitcast.20, bf16[2,32,32,128]{3,2,1,0:T(8,128)(2,1)S(1)} %get-tuple-element.27.emitted, ...), custom_call_target="tpu_custom_call" | custom-call | tf_op jit(solution)/shard_map/pallas_call | solution.py:283
  121.5 0.1 slice_reduce_fusion.1
  121.6 0.6 maximum_log_fusion
  122.2 1.3 %copy.20 = f32[32,32,1,128]{3,2,1,0:T(1,128)} copy(f32[32,32,1,128]{3,0,1,2:T(8,128)S(1)} %bitcast.21) | data formatting | bytes 1048576
  123.5 1.3 %copy.26 = bf16[64,128,128]{2,1,0:T(8,128)(2,1)} copy(bf16[64,128,128]{2,1,0:T(8,128)(2,1)S(1)} %get-tuple-element.31) | data formatting | bytes 4194304
  (4 shorter events, 0.0 us)
Async XLA Ops:
  0.6 3.9 %copy-start = (f32[32,32,1,128]{3,2,1,0:T(1,128)S(1)}, f32[32,32,1,128]{3,2,1,0:T(1,128)}, u32[]{:S(2)}) copy-start(f32[32,32,1,128]{3,2,1,0:T(1,128)} %param.9) | copy-start | bytes 1572868
